TPU v7x, 32 devices: a whole 2x2x4 slice. The times are simulated.
32 devices in a mesh: blk: 16 (over z, x, core), rep: 2 (over y).
Axes of the slice: x: 2, y: 2, z: 4, core: 2. Of those that a mesh axis runs over, the one named last changes fastest.
Arguments:
- image_emb: bfloat16 [16384, 1152], P(('blk', 'rep')), may hold values from -0.19921875 to 0.19921875
- text_emb: bfloat16 [16384, 1152], P(('blk', 'rep')), may hold values from -0.19921875 to 0.19921875
- log_temp: float32 [], replicated, may hold values from 1 to 2
- bias: float32 [], replicated, may hold values from -2 to 0
Outputs:
- row_loss: float32 [16384], P(('blk', 'rep'))
- grad_image: float32 [16384, 1152], P(('blk', 'rep'))
- grad_text: float32 [16384, 1152], P(('blk', 'rep'))
All inputs are finite; a program needn't handle non-finite values.
Results may differ from a plain program's by a relative error of at most 0.0042.
Values may be sent and summed in bfloat16 or wider, within the bound.
A program may use at most 64 MiB of HBM per device.

v0:
```python
import jax
import jax.numpy as jnp
from jax import lax
from jax.sharding import PartitionSpec as P

STEPS = 4


EPSILON = 1e-06


def shifted(x, axis, by):
    count = lax.axis_size(axis)
    return lax.ppermute(x, axis, [(i, (i + by) % count) for i in range(count)])


def unit_rows(embedding):
    values = embedding.astype(jnp.float32)
    scale = lax.rsqrt(jnp.sum(values * values, axis=-1, keepdims=True) + EPSILON)
    return (values * scale, scale)


def block_weights(image_low, partner, temper, bias, labels):
    logits = (
        temper
        * lax.dot_general(
            image_low, partner, (((1,), (1,)), ((), ())), preferred_element_type=jnp.float32
        )
        + bias
    )
    losses = -jnp.sum(jax.nn.log_sigmoid(labels * logits), axis=-1)
    weights = (-labels * jax.nn.sigmoid(-labels * logits) * temper).astype(jnp.bfloat16)
    return (losses, weights)


def block_terms(image_low, partner, temper, bias, labels):
    losses, weights = block_weights(image_low, partner, temper, bias, labels)
    grad_img = jnp.dot(weights, partner, preferred_element_type=jnp.float32)
    grad_txt = lax.dot_general(
        weights, image_low, (((0,), (0,)), ((), ())), preferred_element_type=jnp.float32
    )
    return (losses, grad_img, grad_txt)


def unit_backward(unit, scale, grad_unit):
    return scale * (grad_unit - unit * jnp.sum(unit * grad_unit, axis=-1, keepdims=True))


def body(image_emb, text_emb, log_temp, bias):
    row_count = image_emb.shape[0]
    image_unit, image_scale = unit_rows(image_emb)
    text_unit, text_scale = unit_rows(text_emb)
    image_low = image_unit.astype(jnp.bfloat16)
    text_low = text_unit.astype(jnp.bfloat16)
    temper = jnp.exp(log_temp)
    positive = 2.0 * jnp.eye(row_count, dtype=jnp.float32) - 1.0
    negative = -jnp.ones((row_count, row_count), jnp.float32)
    losses = jnp.zeros((row_count,), jnp.float32)
    grad_img = jnp.zeros(image_unit.shape, jnp.float32)
    partner = text_low
    carried = jnp.zeros(text_unit.shape, jnp.float32)
    for offset in range(STEPS):
        if offset > 0:
            partner = shifted(partner, ("blk", "rep"), 1)
            carried = shifted(carried, ("blk", "rep"), 1)
        labels = positive if offset == 0 else negative
        step_loss, step_img, step_txt = block_terms(image_low, partner, temper, bias, labels)
        losses = losses + step_loss
        grad_img = grad_img + step_img
        carried = carried + step_txt
    grad_txt = shifted(carried, ("blk", "rep"), 1 - STEPS)
    grad_image = unit_backward(image_unit, image_scale, grad_img)
    grad_text = unit_backward(text_unit, text_scale, grad_txt)
    return (losses, grad_image, grad_text)


def solution(mesh):
    return jax.shard_map(
        body,
        mesh=mesh,
        in_specs=(P(("blk", "rep"), None), P(("blk", "rep"), None), P(), P()),
        out_specs=(P(("blk", "rep")), P(("blk", "rep"), None), P(("blk", "rep"), None)),
        check_vma=False,
    )
```

profile of v0, /device:TPU:1, one launch (start us, length us, event | category | flops | bytes accessed | tf_op | source)
XLA Modules:
  0.0 307.2 jit_solution(7263647409246090595)
XLA Ops:
  1.4 1.6 fusion.13
  3.0 1.5 fusion.2
  4.5 0.3 fusion.9
  5.5 1.5 fusion.18
  7.1 1.1 fusion.24
  8.2 2.1 collective-permute-start.3
  10.3 1.7 collective-permute-start
  12.0 75.9 %collective-permute-done = bf16[512,1152]{1,0:T(8,128)(2,1)S(1)} collective-permute-done((bf16[512,1152]{1,0:T(8,128)(2,1)S(1)}, bf16[512,1152]{1,0:T(8,128)(2,1)S(1)}, u32[]{:S(2)}, u32[]{:S(2)}) %collective-permute-start) | collective-permute-done | bytes 1179680 | tf_op jit(solution)/shard_map/ppermute | solution.py:14
  88.0 1.5 fusion.19
  89.5 1.0 convolution_add_fusion
  90.5 0.1 collective-permute-start.4
  90.6 1.4 collective-permute-start.1
  92.0 77.5 %collective-permute-done.1 = bf16[512,1152]{1,0:T(8,128)(2,1)S(1)} collective-permute-done((bf16[512,1152]{1,0:T(8,128)(2,1)S(1)}, bf16[512,1152]{1,0:T(8,128)(2,1)S(1)}, u32[]{:S(2)}, u32[]{:S(2)}) %collective-permute-start.1) | collective-permute-done | bytes 1179680 | tf_op jit(solution)/shard_map/ppermute | solution.py:14
  169.4 1.5 fusion.20
  170.9 1.1 fusion.22
  172.0 0.2 add.110
  172.3 0.1 collective-permute-start.5
  172.4 0.2 collective-permute-start.2
  172.5 78.6 %collective-permute-done.2 = bf16[512,1152]{1,0:T(8,128)(2,1)S(1)} collective-permute-done((bf16[512,1152]{1,0:T(8,128)(2,1)S(1)}, bf16[512,1152]{1,0:T(8,128)(2,1)S(1)}, u32[]{:S(2)}, u32[]{:S(2)}) %collective-permute-start.2) | collective-permute-done | bytes 1179680 | tf_op jit(solution)/shard_map/ppermute | solution.py:14
  251.2 1.5 fusion.21
  252.7 1.1 fusion.23
  253.8 0.2 add.111
  254.0 1.9 collective-permute-start.6
  256.0 0.9 fusion.25
  256.9 0.9 convolution_add_fusion.3
  257.8 0.9 convolution_add_fusion.2
  258.8 0.6 add_add_fusion
  259.3 1.2 fusion.6
  260.6 1.9 fusion.8
  262.5 42.4 %collective-permute-done.6 = f32[512,1152]{1,0:T(8,128)S(1)} collective-permute-done((f32[512,1152]{1,0:T(8,128)S(1)}, f32[512,1152]{1,0:T(8,128)S(1)}, u32[]{:S(2)}, u32[]{:S(2)}) %collective-permute-start.6) | collective-permute-done | bytes 2359328 | tf_op jit(solution)/shard_map/ppermute | solution.py:14
  304.8 0.5 fusion.10
  305.3 1.9 fusion.12
  (9 shorter events, 0.0 us)
Async XLA Ops:
  0.6 3.9 %copy-start.1 = (bf16[512,1152]{1,0:T(8,128)(2,1)S(1)}, bf16[512,1152]{1,0:T(8,128)(2,1)}, u32[]{:S(2)}) copy-start(bf16[512,1152]{1,0:T(8,128)(2,1)} %param.4) | copy-start | bytes 3538948
  8.2 81.3 %collective-permute-start.3 = (f32[512,1152]{1,0:T(8,128)S(1)}, f32[512,1152]{1,0:T(8,128)S(1)}, u32[]{:S(2)}, u32[]{:S(2)}) collective-permute-start(f32[512,1152]{1,0:T(8,128)S(1)} %fusion.24), channel_id=1, source_target_pairs={{0,1},{1,2},{2,3},{3,4},{4,5},{5,6},{6,7},{7,8},{8,9},{9,10},{10,1... | collective-permute-start | bytes 7077896 | tf_op jit(solution)/shard_map/ppermute | solution.py:14
  10.3 77.6 %collective-permute-start = (bf16[512,1152]{1,0:T(8,128)(2,1)S(1)}, bf16[512,1152]{1,0:T(8,128)(2,1)S(1)}, u32[]{:S(2)}, u32[]{:S(2)}) collective-permute-start(bf16[512,1152]{1,0:T(8,128)(2,1)S(1)} %fusion.2), channel_id=1, source_target_pairs={{0,1},{1,2},{2,3},{3,4},{4,5},{5,6},{6,7},{7,8},{8,9},{9,10},{10,1... | collective-permute-start | bytes 3538952 | tf_op jit(solution)/shard_map/ppermute | solution.py:14
  90.5 81.5 %collective-permute-start.4 = (f32[512,1152]{1,0:T(8,128)S(1)}, f32[512,1152]{1,0:T(8,128)S(1)}, u32[]{:S(2)}, u32[]{:S(2)}) collective-permute-start(f32[512,1152]{1,0:T(8,128)S(1)} %convolution_add_fusion), channel_id=1, source_target_pairs={{0,1},{1,2},{2,3},{3,4},{4,5},{5,6},{6,7},{7,8},{8,9},{9,10},{10,1... | collective-permute-start | bytes 7077896 | tf_op jit(solution)/shard_map/ppermute | solution.py:14
  90.6 78.8 %collective-permute-start.1 = (bf16[512,1152]{1,0:T(8,128)(2,1)S(1)}, bf16[512,1152]{1,0:T(8,128)(2,1)S(1)}, u32[]{:S(2)}, u32[]{:S(2)}) collective-permute-start(bf16[512,1152]{1,0:T(8,128)(2,1)S(1)} %collective-permute-done), channel_id=1, source_target_pairs={{0,1},{1,2},{2,3},{3,4},{4,5},{5,6},{6,7},{7,8},{8,9},{9,10},{10,1... | collective-permute-start | bytes 3538952 | tf_op jit(solution)/shard_map/ppermute | solution.py:14
  172.3 81.5 %collective-permute-start.5 = (f32[512,1152]{1,0:T(8,128)S(1)}, f32[512,1152]{1,0:T(8,128)S(1)}, u32[]{:S(2)}, u32[]{:S(2)}) collective-permute-start(f32[512,1152]{1,0:T(8,128)S(1)} %add.110), channel_id=1, source_target_pairs={{0,1},{1,2},{2,3},{3,4},{4,5},{5,6},{6,7},{7,8},{8,9},{9,10},{10,1... | collective-permute-start | bytes 7077896 | tf_op jit(solution)/shard_map/ppermute | solution.py:14
  172.4 78.8 %collective-permute-start.2 = (bf16[512,1152]{1,0:T(8,128)(2,1)S(1)}, bf16[512,1152]{1,0:T(8,128)(2,1)S(1)}, u32[]{:S(2)}, u32[]{:S(2)}) collective-permute-start(bf16[512,1152]{1,0:T(8,128)(2,1)S(1)} %collective-permute-done.1), channel_id=1, source_target_pairs={{0,1},{1,2},{2,3},{3,4},{4,5},{5,6},{6,7},{7,8},{8,9},{9,10},{10,1... | collective-permute-start | bytes 3538952 | tf_op jit(solution)/shard_map/ppermute | solution.py:14
  254.0 50.8 %collective-permute-start.6 = (f32[512,1152]{1,0:T(8,128)S(1)}, f32[512,1152]{1,0:T(8,128)S(1)}, u32[]{:S(2)}, u32[]{:S(2)}) collective-permute-start(f32[512,1152]{1,0:T(8,128)S(1)} %add.111), channel_id=1, source_target_pairs={{0,29},{1,30},{2,31},{3,0},{4,1},{5,2},{6,3},{7,4},{8,5},{9,6},{10... | collective-permute-start | bytes 7077896 | tf_op jit(solution)/shard_map/ppermute | solution.py:14
  260.6 44.3 %copy-start = (bf16[512,1152]{1,0:T(8,128)(2,1)S(1)}, bf16[512,1152]{1,0:T(8,128)(2,1)}, u32[]{:S(2)}) copy-start(bf16[512,1152]{1,0:T(8,128)(2,1)} %param.5) | copy-start | bytes 3538948
where the time goes:
time: 310 us; the launch traced here: 307 us
  waiting for transfers between devices  274 us (88%)
  matrix products  14.4 us (5%)
  other arithmetic  8.7 us (3%)
  starting transfers between devices  7.46 us (2%)
    ppermute x7, waiting for transfers between devices, shifted(): return lax.ppermute(x, axis, [(i, (i + by) % count) for i in range(count)])  274 us
    ppermute x7, starting transfers between devices, shifted(): return lax.ppermute(x, axis, [(i, (i + by) % count) for i in range(count)])  7.46 us
  transfers between devices with their start and end apart: 7, of which 4 were waited for; matrix products, arithmetic and copies ran while one was open for 4% of the time, Pallas kernels for 0%

commit v1 on v0

v1 whole, which is shorter than its diff:
```python
import functools

import jax
import jax.numpy as jnp
from jax import lax
from jax.experimental import pallas as pl
from jax.experimental.pallas import tpu as pltpu
from jax.sharding import PartitionSpec as P

EPSILON = 1e-06
MESH = pl.DeviceIdType.MESH
CHUNKS = 4
HALVES = 2
NT = (((1,), (1,)), ((), ()))


def row_scale(values):
    return lax.rsqrt(jnp.sum(values * values, axis=-1, keepdims=True) + EPSILON)


def kernel(
    count,
    reps,
    log_temp,
    bias,
    image_emb,
    text_emb,
    loss_out,
    grad_image,
    grad_text,
    image_low,
    text_low,
    texts,
    images,
    loss_acc,
    send_sem,
    text_sem,
    image_sem,
):
    rows, width = image_emb.shape
    piece = rows // CHUNKS
    half = rows // HALVES
    me = lax.axis_index("blk") * reps + lax.axis_index("rep")
    place = lax.rem(me, 4)

    def device(by):
        index = lax.rem(me + by + count, count)
        return (index // reps, lax.rem(index, reps))

    barrier = pltpu.get_barrier_semaphore()
    for by in (-2, -1, 1, 2):
        pl.semaphore_signal(barrier, inc=1, device_id=device(by), device_id_type=MESH)

    def normalise(emb, low, c):
        part = pl.ds(c * piece, piece)
        values = emb[part, :].astype(jnp.float32)
        low[part, :] = (values * row_scale(values)).astype(jnp.bfloat16)

    def copy(kind, c, src, dst, sem, by):
        part = pl.ds(c * piece, piece)
        return pltpu.make_async_remote_copy(
            src_ref=src.at[part, :],
            dst_ref=dst.at[part, :],
            send_sem=send_sem.at[kind, c],
            recv_sem=sem,
            device_id=device(by),
            device_id_type=MESH,
        )

    def text_two(c):
        return copy(0, c, text_low, texts.at[1], text_sem.at[1, c], 2)

    def image_two(c):
        return copy(1, c, image_low, images.at[1], image_sem.at[1, c], -2)

    def text_one(c):
        return copy(2, c, text_low, texts.at[0], text_sem.at[0, c], 1)

    def image_one(c):
        return copy(3, c, image_low, images.at[0], image_sem.at[0, c], -1)

    def text_turn(c):
        return copy(4, c, texts.at[1], texts.at[0], text_sem.at[0, c], -1)

    def image_turn(c):
        return copy(5, c, images.at[1], images.at[0], image_sem.at[0, c], 1)

    def text_three(c):
        return copy(6, c, texts.at[0], texts.at[2], text_sem.at[2, c], 2)

    def image_three(c):
        return copy(7, c, images.at[0], images.at[2], image_sem.at[2, c], -2)

    def got_text(j, c):
        copy(0, c, text_low, texts.at[j], text_sem.at[j, c], 2).wait_recv()

    def got_image(j, c):
        copy(1, c, image_low, images.at[j], image_sem.at[j, c], -2).wait_recv()

    normalise(text_emb, text_low, 0)
    normalise(image_emb, image_low, 0)
    pl.semaphore_wait(barrier, 4)
    for c in range(CHUNKS):
        if c > 0:
            normalise(text_emb, text_low, c)
            normalise(image_emb, image_low, c)

        @pl.when(place != 3)
        def _():
            text_one(c).start()

        @pl.when(place != 0)
        def _():
            image_one(c).start()

        text_two(c).start()
        image_two(c).start()

    temper = jnp.exp(jnp.full((1, half), log_temp[0], jnp.float32))
    slope = 0.5 * temper
    shift = jnp.full((1, half), 0.5 * bias[0], jnp.float32)
    grad_image[...] = jnp.zeros_like(grad_image)
    grad_text[...] = jnp.zeros_like(grad_text)
    loss_acc[...] = jnp.zeros_like(loss_acc)

    def step(own, other, acc, h, diagonal, with_loss):
        block = other[pl.ds(h * half, half), :]

        @pl.loop(0, HALVES)
        def _(m):
            part = pl.ds(pl.multiple_of(m * half, half), half)
            dots = lax.dot_general(own[part, :], block, NT, preferred_element_type=jnp.float32)
            turn = jnp.tanh(dots * slope + shift)
            weights = slope + slope * turn
            other_side = 0.5 - 0.5 * turn
            if diagonal:
                row = lax.broadcasted_iota(jnp.int32, (half, half), 0)
                column = lax.broadcasted_iota(jnp.int32, (half, half), 1)
                positive = row + m * half == column + h * half
                weights = jnp.where(positive, slope * turn - slope, weights)
                other_side = jnp.where(positive, 0.5 + 0.5 * turn, other_side)
            if with_loss:
                product = other_side[:, :128]
                for at in range(128, half, 128):
                    product = product * other_side[:, at : at + 128]
                loss_acc[part, :] -= jnp.log(product)
            acc[part, :] += jnp.dot(
                weights.astype(jnp.bfloat16), block, preferred_element_type=jnp.float32
            )

    def image_step(other, h, diagonal=False):
        step(image_low, other, grad_image, h, diagonal, True)

    def text_step(other, h, diagonal=False):
        step(text_low, other, grad_text, h, diagonal, False)

    def pass_text(c):
        got_text(0, c)
        text_three(c).start()

    def pass_image(c):
        got_image(0, c)
        image_three(c).start()

    def arrivals(c):
        got_text(1, c)

        @pl.when(place == 1)
        def _():
            text_turn(c).start()

        got_image(1, c)

        @pl.when(place == 2)
        def _():
            image_turn(c).start()

        @pl.when(place == 0)
        def _():
            pass_image(c)
            if c > 0:
                pass_text(c - 1)

        @pl.when(place == 3)
        def _():
            pass_text(c)
            if c > 0:
                pass_image(c - 1)

        @pl.when(jnp.logical_and(place != 0, place != 3))
        def _():
            pass_text(c)
            pass_image(c)

    for h in range(HALVES):
        image_step(text_low, h, True)
        text_step(image_low, h, True)
    per = CHUNKS // HALVES
    for h in range(HALVES):
        for c in range(h * per, (h + 1) * per):
            arrivals(c)
        if h == HALVES - 1:

            @pl.when(place == 0)
            def _():
                pass_text(CHUNKS - 1)

            @pl.when(place == 3)
            def _():
                pass_image(CHUNKS - 1)

        image_step(texts.at[1], h)
        text_step(images.at[1], h)
        if h > 0:
            image_step(texts.at[0], h - 1)
            text_step(images.at[0], h - 1)
    image_step(texts.at[0], HALVES - 1)
    text_step(images.at[0], HALVES - 1)
    for h in range(HALVES):
        for c in range(h * per, (h + 1) * per):
            got_text(2, c)
            got_image(2, c)
        image_step(texts.at[2], h)
        text_step(images.at[2], h)

    def finish(emb, acc):
        @pl.loop(0, CHUNKS)
        def _(c):
            part = pl.ds(pl.multiple_of(c * piece, piece), piece)
            values = emb[part, :].astype(jnp.float32)
            scale = row_scale(values)
            unit = values * scale
            grad = acc[part, :]
            acc[part, :] = scale * (grad - unit * jnp.sum(unit * grad, axis=-1, keepdims=True))

    finish(image_emb, grad_image)
    finish(text_emb, grad_text)
    for at in range(rows // 128):
        part = loss_acc[at * 128 : (at + 1) * 128, :]
        loss_out[at : at + 1, :] = jnp.sum(part.T, axis=0, keepdims=True)

    for c in range(CHUNKS):
        text_two(c).wait_send()
        image_two(c).wait_send()
        text_three(c).wait_send()
        image_three(c).wait_send()

        @pl.when(place != 3)
        def _():
            text_one(c).wait_send()

        @pl.when(place != 0)
        def _():
            image_one(c).wait_send()

        @pl.when(place == 1)
        def _():
            text_turn(c).wait_send()

        @pl.when(place == 2)
        def _():
            image_turn(c).wait_send()


def body(count, reps, image_emb, text_emb, log_temp, bias):
    rows, width = image_emb.shape
    vmem = pl.BlockSpec(memory_space=pltpu.VMEM)
    smem = pl.BlockSpec(memory_space=pltpu.SMEM)
    losses, grad_image, grad_text = pl.pallas_call(
        functools.partial(kernel, count, reps),
        out_shape=(
            jax.ShapeDtypeStruct((rows // 128, 128), jnp.float32),
            jax.ShapeDtypeStruct((rows, width), jnp.float32),
            jax.ShapeDtypeStruct((rows, width), jnp.float32),
        ),
        in_specs=[smem, smem, vmem, vmem],
        out_specs=(vmem, vmem, vmem),
        scratch_shapes=[
            pltpu.VMEM((rows, width), jnp.bfloat16),
            pltpu.VMEM((rows, width), jnp.bfloat16),
            pltpu.VMEM((3, rows, width), jnp.bfloat16),
            pltpu.VMEM((3, rows, width), jnp.bfloat16),
            pltpu.VMEM((rows, 128), jnp.float32),
            pltpu.SemaphoreType.DMA((8, CHUNKS)),
            pltpu.SemaphoreType.DMA((3, CHUNKS)),
            pltpu.SemaphoreType.DMA((3, CHUNKS)),
        ],
        compiler_params=pltpu.CompilerParams(
            collective_id=0, has_side_effects=True, vmem_limit_bytes=44 * 1024 * 1024
        ),
        cost_estimate=pl.CostEstimate(
            flops=32 * rows * rows * width,
            bytes_accessed=12 * rows * width,
            transcendentals=14 * rows * rows,
        ),
    )(log_temp.reshape(1), bias.reshape(1), image_emb, text_emb)
    return losses.reshape(rows), grad_image, grad_text


def solution(mesh):
    reps = mesh.shape["rep"]
    count = mesh.shape["blk"] * reps
    return jax.shard_map(
        functools.partial(body, count, reps),
        mesh=mesh,
        in_specs=(P(("blk", "rep"), None), P(("blk", "rep"), None), P(), P()),
        out_specs=(P(("blk", "rep")), P(("blk", "rep"), None), P(("blk", "rep"), None)),
        check_vma=False,
    )
```

time: 310 us -> 86.1 us (0.28)
  the two profiles are of different devices: /device:TPU:1 before, /device:TPU:0 now
where the time goes in v1:
time: 86.1 us; the launch traced here: 85.9 us
  Pallas kernels  78.1 us (91%)
  local copies, waits for them, and re-layouts  5.92 us (7%)
  between operations  1.94 us (2%)
    pallas_call x1, Pallas kernels, body(): pl.pallas_call(functools.partial(kernel, count, reps), out_shape=(jax.Sha...  78.1 us
    unnamed x7, local copies, waits for them, and re-layouts  5.92 us

profile of v1, /device:TPU:0, one launch (start us, length us, event | category | flops | bytes accessed | tf_op | source)
XLA Modules:
  0.0 85.9 jit_solution(14346330048813702265)
XLA Ops:
  1.9 0.0 copy-start
  1.9 1.3 %copy-done = bf16[512,1152]{1,0:T(8,128)(2,1)S(1)} copy-done((bf16[512,1152]{1,0:T(8,128)(2,1)S(1)}, bf16[512,1152]{1,0:T(8,128)(2,1)}, u32[]{:S(2)}) %copy-start) | copy-done | bytes 1179672
  3.2 0.0 copy-start.1
  3.2 1.3 %copy-done.1 = bf16[512,1152]{1,0:T(8,128)(2,1)S(1)} copy-done((bf16[512,1152]{1,0:T(8,128)(2,1)S(1)}, bf16[512,1152]{1,0:T(8,128)(2,1)}, u32[]{:S(2)}) %copy-start.1) | copy-done | bytes 1179672
  4.5 78.1 %shard_map.67 = (f32[4,128]{1,0:T(4,128)S(1)}, f32[512,1152]{1,0:T(8,128)S(1)}, f32[512,1152]{1,0:T(8,128)S(1)}) custom-call(f32[1]{0:T(128)} %bitcast.3.log_temp, f32[1]{0:T(128)} %bitcast.4.bias, bf16[512,1152]{1,0:T(8,128)(2,1)S(1)} %copy-done, bf16[512,1152]{1,0:T(8,128)(2,1)S(1)} %copy-done.1), custom_call_target="tpu_custom_call" | custom-call | flops 9663676416 | bytes 7077888 | tf_op jit(solution)/shard_map/pallas_call | solution.py:269
  82.5 0.6 copy.12
  83.1 1.4 %copy.13 = f32[512,1152]{1,0:T(8,128)} copy(f32[512,1152]{1,0:T(8,128)S(1)} %get-tuple-element.13) | data formatting | bytes 4718592
  84.5 1.4 %copy.14 = f32[512,1152]{1,0:T(8,128)} copy(f32[512,1152]{1,0:T(8,128)S(1)} %get-tuple-element.14) | data formatting | bytes 4718592
Async XLA Ops:
  1.9 1.3 %copy-start = (bf16[512,1152]{1,0:T(8,128)(2,1)S(1)}, bf16[512,1152]{1,0:T(8,128)(2,1)}, u32[]{:S(2)}) copy-start(bf16[512,1152]{1,0:T(8,128)(2,1)} %image_emb.1) | copy-start | bytes 3538948
  3.2 1.3 %copy-start.1 = (bf16[512,1152]{1,0:T(8,128)(2,1)S(1)}, bf16[512,1152]{1,0:T(8,128)(2,1)}, u32[]{:S(2)}) copy-start(bf16[512,1152]{1,0:T(8,128)(2,1)} %text_emb.1) | copy-start | bytes 3538948

commit v2 on v1

v2 whole, which is shorter than its diff:
```python
import functools

import jax
import jax.numpy as jnp
from jax import lax
from jax.experimental import pallas as pl
from jax.experimental.pallas import tpu as pltpu
from jax.sharding import PartitionSpec as P

EPSILON = 1e-06
MESH = pl.DeviceIdType.MESH
CHUNKS = 4
HALVES = 2
NT = (((1,), (1,)), ((), ()))


def row_scale(values):
    return lax.rsqrt(jnp.sum(values * values, axis=-1, keepdims=True) + EPSILON)


def kernel(
    blocks,
    log_temp,
    bias,
    image_emb,
    text_emb,
    loss_out,
    grad_image,
    grad_text,
    image_held,
    text_held,
    image_low,
    text_low,
    texts,
    images,
    loss_acc,
    fetch_sem,
    send_sem,
    text_sem,
    image_sem,
):
    rows, width = image_emb.shape
    piece = rows // CHUNKS
    half = rows // HALVES
    blk, rep = lax.axis_index("blk"), lax.axis_index("rep")
    ahead = (lax.rem(blk + 1, blocks), rep)
    behind = (lax.rem(blk + blocks - 1, blocks), rep)
    across = (blk, 1 - rep)
    core = lax.rem(blk, 2)

    def chunk(c):
        return pl.ds(c * piece, piece)

    def fetch(kind, emb, held, c):
        return pltpu.make_async_copy(
            emb.at[chunk(c), :], held.at[chunk(c), :], fetch_sem.at[kind, c]
        )

    for c in range(CHUNKS):
        fetch(0, text_emb, text_held, c).start()
        fetch(1, image_emb, image_held, c).start()
    barrier = pltpu.get_barrier_semaphore()
    for other in (ahead, behind, across):
        pl.semaphore_signal(barrier, inc=1, device_id=other, device_id_type=MESH)

    def normalise(held, low, c):
        values = held[chunk(c), :].astype(jnp.float32)
        low[chunk(c), :] = (values * row_scale(values)).astype(jnp.bfloat16)

    def prepare(c):
        fetch(0, text_emb, text_held, c).wait()
        normalise(text_held, text_low, c)
        fetch(1, image_emb, image_held, c).wait()
        normalise(image_held, image_low, c)

    def copy(kind, c, src, dst, sem, to):
        return pltpu.make_async_remote_copy(
            src_ref=src.at[chunk(c), :],
            dst_ref=dst.at[chunk(c), :],
            send_sem=send_sem.at[kind, c],
            recv_sem=sem,
            device_id=to,
            device_id_type=MESH,
        )

    def text_two(c):
        return copy(0, c, text_low, texts.at[1], text_sem.at[1, c], ahead)

    def image_two(c):
        return copy(1, c, image_low, images.at[1], image_sem.at[1, c], behind)

    def text_three(c):
        return copy(2, c, texts.at[0], texts.at[2], text_sem.at[2, c], ahead)

    def image_three(c):
        return copy(3, c, images.at[0], images.at[2], image_sem.at[2, c], behind)

    def text_one(c):
        return copy(4, c, text_low, texts.at[0], text_sem.at[0, c], across)

    def image_turn(c):
        return copy(5, c, images.at[1], images.at[0], image_sem.at[0, c], across)

    def image_one(c):
        return copy(4, c, image_low, images.at[0], image_sem.at[0, c], across)

    def text_turn(c):
        return copy(5, c, texts.at[1], texts.at[0], text_sem.at[0, c], across)

    def got_text(j, c):
        copy(0, c, text_low, texts.at[j], text_sem.at[j, c], ahead).wait_recv()

    def got_image(j, c):
        copy(1, c, image_low, images.at[j], image_sem.at[j, c], behind).wait_recv()

    def pass_text(c):
        got_text(0, c)
        text_three(c).start()

    def pass_image(c):
        got_image(0, c)
        image_three(c).start()

    first, second = core == 0, core == 1
    even, odd = rep == 0, rep == 1

    def on(*conditions):
        return pl.when(functools.reduce(jnp.logical_and, conditions))

    prepare(0)
    pl.semaphore_wait(barrier, 3)
    for c in range(CHUNKS):
        if c > 0:
            prepare(c)
        text_two(c).start()
        image_two(c).start()

        @on(even, second)
        def _():
            text_one(c).start()

        @on(odd, first)
        def _():
            image_one(c).start()

    @on(even, first)
    def _():
        for c in range(CHUNKS):
            got_image(1, c)
            image_turn(c).start()
        for c in range(CHUNKS):
            text_one(c).start()

    @on(odd, second)
    def _():
        for c in range(CHUNKS):
            got_text(1, c)
            text_turn(c).start()
        for c in range(CHUNKS):
            image_one(c).start()

    temper = jnp.exp(jnp.full((1, half), log_temp[0], jnp.float32))
    slope = 0.5 * temper
    shift = jnp.full((1, half), 0.5 * bias[0], jnp.float32)
    grad_image[...] = jnp.zeros_like(grad_image)
    grad_text[...] = jnp.zeros_like(grad_text)
    loss_acc[...] = jnp.zeros_like(loss_acc)

    def step(own, other, acc, h, diagonal, with_loss):
        block = other[pl.ds(h * half, half), :]

        @pl.loop(0, HALVES)
        def _(m):
            part = pl.ds(pl.multiple_of(m * half, half), half)
            dots = lax.dot_general(own[part, :], block, NT, preferred_element_type=jnp.float32)
            turn = jnp.tanh(dots * slope + shift)
            weights = slope + slope * turn
            other_side = 0.5 - 0.5 * turn
            if diagonal:
                row = lax.broadcasted_iota(jnp.int32, (half, half), 0)
                column = lax.broadcasted_iota(jnp.int32, (half, half), 1)
                positive = row + m * half == column + h * half
                weights = jnp.where(positive, slope * turn - slope, weights)
                other_side = jnp.where(positive, 0.5 + 0.5 * turn, other_side)
            if with_loss:
                product = other_side[:, :128]
                for at in range(128, half, 128):
                    product = product * other_side[:, at : at + 128]
                loss_acc[part, :] -= jnp.log(product)
            acc[part, :] += jnp.dot(
                weights.astype(jnp.bfloat16), block, preferred_element_type=jnp.float32
            )

    def image_step(other, h, diagonal=False):
        step(image_low, other, grad_image, h, diagonal, True)

    def text_step(other, h, diagonal=False):
        step(text_low, other, grad_text, h, diagonal, False)

    def early(c):
        @on(first)
        def _():
            pass_image(c)
            got_text(1, c)

        @on(first, odd)
        def _():
            text_turn(c).start()
            got_image(1, c)

        @on(second)
        def _():
            pass_text(c)
            got_image(1, c)

        @on(second, even)
        def _():
            image_turn(c).start()
            got_text(1, c)

    def late(c):
        @on(first)
        def _():
            pass_text(c)

        @on(second)
        def _():
            pass_image(c)

    for h in range(HALVES):
        image_step(text_low, h, True)
        text_step(image_low, h, True)
    per = CHUNKS // HALVES
    for h in range(HALVES):
        for c in range(h * per, (h + 1) * per):
            early(c)
            if c > 0:
                late(c - 1)
            if h > 0 and c == h * per:
                image_step(texts.at[0], h - 1)
                text_step(images.at[0], h - 1)
        image_step(texts.at[1], h)
        text_step(images.at[1], h)
    late(CHUNKS - 1)
    image_step(texts.at[0], HALVES - 1)
    text_step(images.at[0], HALVES - 1)
    for h in range(HALVES):
        for c in range(h * per, (h + 1) * per):
            got_text(2, c)
            got_image(2, c)
        image_step(texts.at[2], h)
        text_step(images.at[2], h)

    def finish(held, acc):
        @pl.loop(0, CHUNKS)
        def _(c):
            part = pl.ds(pl.multiple_of(c * piece, piece), piece)
            values = held[part, :].astype(jnp.float32)
            scale = row_scale(values)
            unit = values * scale
            grad = acc[part, :]
            acc[part, :] = scale * (grad - unit * jnp.sum(unit * grad, axis=-1, keepdims=True))

    finish(image_held, grad_image)
    finish(text_held, grad_text)
    for at in range(rows // 128):
        part = loss_acc[at * 128 : (at + 1) * 128, :]
        loss_out[at : at + 1, :] = jnp.sum(part.T, axis=0, keepdims=True)

    for c in range(CHUNKS):
        text_two(c).wait_send()
        image_two(c).wait_send()
        text_three(c).wait_send()
        image_three(c).wait_send()

        @on(even)
        def _():
            text_one(c).wait_send()
            image_turn(c).wait_send()

        @on(odd)
        def _():
            image_one(c).wait_send()
            text_turn(c).wait_send()


def body(blocks, image_emb, text_emb, log_temp, bias):
    rows, width = image_emb.shape
    vmem = pl.BlockSpec(memory_space=pltpu.VMEM)
    hbm = pl.BlockSpec(memory_space=pltpu.HBM)
    smem = pl.BlockSpec(memory_space=pltpu.SMEM)
    losses, grad_image, grad_text = pl.pallas_call(
        functools.partial(kernel, blocks),
        out_shape=(
            jax.ShapeDtypeStruct((rows // 128, 128), jnp.float32),
            jax.ShapeDtypeStruct((rows, width), jnp.float32),
            jax.ShapeDtypeStruct((rows, width), jnp.float32),
        ),
        in_specs=[smem, smem, hbm, hbm],
        out_specs=(vmem, vmem, vmem),
        scratch_shapes=[
            pltpu.VMEM((rows, width), jnp.bfloat16),
            pltpu.VMEM((rows, width), jnp.bfloat16),
            pltpu.VMEM((rows, width), jnp.bfloat16),
            pltpu.VMEM((rows, width), jnp.bfloat16),
            pltpu.VMEM((3, rows, width), jnp.bfloat16),
            pltpu.VMEM((3, rows, width), jnp.bfloat16),
            pltpu.VMEM((rows, 128), jnp.float32),
            pltpu.SemaphoreType.DMA((2, CHUNKS)),
            pltpu.SemaphoreType.DMA((6, CHUNKS)),
            pltpu.SemaphoreType.DMA((3, CHUNKS)),
            pltpu.SemaphoreType.DMA((3, CHUNKS)),
        ],
        compiler_params=pltpu.CompilerParams(
            collective_id=0, has_side_effects=True, vmem_limit_bytes=44 * 1024 * 1024
        ),
        cost_estimate=pl.CostEstimate(
            flops=32 * rows * rows * width,
            bytes_accessed=12 * rows * width,
            transcendentals=14 * rows * rows,
        ),
    )(log_temp.reshape(1), bias.reshape(1), image_emb, text_emb)
    return losses.reshape(rows), grad_image, grad_text


def solution(mesh):
    if mesh.shape["rep"] != 2 or mesh.shape["blk"] % 2:
        raise ValueError("mesh")
    return jax.shard_map(
        functools.partial(body, mesh.shape["blk"]),
        mesh=mesh,
        in_specs=(P(("blk", "rep"), None), P(("blk", "rep"), None), P(), P()),
        out_specs=(P(("blk", "rep")), P(("blk", "rep"), None), P(("blk", "rep"), None)),
        check_vma=False,
    )
```

time: 86.1 us -> 81.4 us (0.945)
  the two profiles are of different devices: /device:TPU:0 before, /device:TPU:1 now
where the time goes in v2:
time: 81.4 us; the launch traced here: 81.2 us
  Pallas kernels  73.3 us (90%)
  local copies, waits for them, and re-layouts  5.92 us (7%)
  between operations  1.94 us (2%)
    pallas_call x1, Pallas kernels, body(): pl.pallas_call(functools.partial(kernel, blocks), out_shape=(jax.ShapeDty...  73.3 us
    unnamed x7, local copies, waits for them, and re-layouts  5.92 us

profile of v2, /device:TPU:1, one launch (start us, length us, event | category | flops | bytes accessed | tf_op | source)
XLA Modules:
  0.0 81.2 jit_solution(14695631215808664804)
XLA Ops:
  1.9 0.0 copy-start
  1.9 1.3 %copy-done = bf16[512,1152]{1,0:T(8,128)(2,1)S(1)} copy-done((bf16[512,1152]{1,0:T(8,128)(2,1)S(1)}, bf16[512,1152]{1,0:T(8,128)(2,1)}, u32[]{:S(2)}) %copy-start) | copy-done | bytes 1179672
  3.2 0.0 copy-start.1
  3.2 1.3 %copy-done.1 = bf16[512,1152]{1,0:T(8,128)(2,1)S(1)} copy-done((bf16[512,1152]{1,0:T(8,128)(2,1)S(1)}, bf16[512,1152]{1,0:T(8,128)(2,1)}, u32[]{:S(2)}) %copy-start.1) | copy-done | bytes 1179672
  4.5 73.3 %shard_map.67 = (f32[4,128]{1,0:T(4,128)S(1)}, f32[512,1152]{1,0:T(8,128)S(1)}, f32[512,1152]{1,0:T(8,128)S(1)}) custom-call(f32[1]{0:T(128)} %bitcast.3.log_temp, f32[1]{0:T(128)} %bitcast.4.bias, bf16[512,1152]{1,0:T(8,128)(2,1)S(1)} %copy-done, bf16[512,1152]{1,0:T(8,128)(2,1)S(1)} %copy-done.1), custom_call_target="tpu_custom_call" | custom-call | flops 9663676416 | bytes 7077888 | tf_op jit(solution)/shard_map/pallas_call | solution.py:292
  77.8 0.6 copy.12
  78.4 1.4 %copy.13 = f32[512,1152]{1,0:T(8,128)} copy(f32[512,1152]{1,0:T(8,128)S(1)} %get-tuple-element.13) | data formatting | bytes 4718592
  79.8 1.4 %copy.14 = f32[512,1152]{1,0:T(8,128)} copy(f32[512,1152]{1,0:T(8,128)S(1)} %get-tuple-element.14) | data formatting | bytes 4718592
Async XLA Ops:
  1.9 1.3 %copy-start = (bf16[512,1152]{1,0:T(8,128)(2,1)S(1)}, bf16[512,1152]{1,0:T(8,128)(2,1)}, u32[]{:S(2)}) copy-start(bf16[512,1152]{1,0:T(8,128)(2,1)} %image_emb.1) | copy-start | bytes 3538948
  3.2 1.3 %copy-start.1 = (bf16[512,1152]{1,0:T(8,128)(2,1)S(1)}, bf16[512,1152]{1,0:T(8,128)(2,1)}, u32[]{:S(2)}) copy-start(bf16[512,1152]{1,0:T(8,128)(2,1)} %text_emb.1) | copy-start | bytes 3538948

commit v3 on v0

v3 whole, which is shorter than its diff:
```python
import functools

import jax
import jax.numpy as jnp
from jax import lax
from jax.experimental import pallas as pl
from jax.experimental.pallas import tpu as pltpu
from jax.sharding import PartitionSpec as P

EPSILON = 1e-06
MESH = pl.DeviceIdType.MESH
CHUNKS = 4
HALVES = 2
NT = (((1,), (1,)), ((), ()))


def row_scale(values):
    return lax.rsqrt(jnp.sum(values * values, axis=-1, keepdims=True) + EPSILON)


def kernel(
    blocks,
    log_temp,
    bias,
    image_emb,
    text_emb,
    loss_out,
    grads,
    held,
    low,
    came,
    loss_acc,
    fetch_sem,
    send_sem,
    came_sem,
):
    rows, width = image_emb.shape
    piece = rows // CHUNKS
    half = rows // HALVES
    blk, rep = lax.axis_index("blk"), lax.axis_index("rep")
    core = lax.rem(blk, 2)
    mate = (blk + 1 - 2 * core, rep)
    far = (lax.rem(blk + blocks - 1 + 2 * core, blocks), rep)
    across = (blk, 1 - rep)
    outer, inner = 1 - core, core
    straight, turned = rep == outer, rep != outer

    def chunk(c):
        return pl.ds(c * piece, piece)

    def fetch(side, c):
        emb = text_emb if side else image_emb
        return pltpu.make_async_copy(
            emb.at[chunk(c), :], held.at[side, chunk(c), :], fetch_sem.at[side, c]
        )

    for c in range(CHUNKS):
        fetch(0, c).start()
        fetch(1, c).start()
    barrier = pltpu.get_barrier_semaphore()
    for other in (mate, far, across):
        pl.semaphore_signal(barrier, inc=1, device_id=other, device_id_type=MESH)

    def prepare(c):
        for side in range(2):
            fetch(side, c).wait()
            values = held[side, chunk(c), :].astype(jnp.float32)
            low[side, chunk(c), :] = (values * row_scale(values)).astype(jnp.bfloat16)

    def copy(kind, c, src, side, j, to):
        return pltpu.make_async_remote_copy(
            src_ref=src.at[chunk(c), :],
            dst_ref=came.at[side, j, chunk(c), :],
            send_sem=send_sem.at[kind, c],
            recv_sem=came_sem.at[side, j, c],
            device_id=to,
            device_id_type=MESH,
        )

    def far_own(c):
        return copy(0, c, low.at[1 - outer], outer, 1, far)

    def mate_own(c):
        return copy(1, c, low.at[1 - inner], inner, 1, mate)

    def far_pass(c):
        return copy(2, c, came.at[outer, 0], outer, 2, far)

    def mate_pass(c):
        return copy(3, c, came.at[inner, 0], inner, 2, mate)

    def across_own(c):
        return copy(4, c, low.at[1 - rep], rep, 0, across)

    def across_turn(c):
        return copy(5, c, came.at[1 - rep, 1], 1 - rep, 0, across)

    def got(side, j, c):
        copy(0, c, low.at[0], side, j, far).wait_recv()

    prepare(0)
    pl.semaphore_wait(barrier, 3)
    for c in range(CHUNKS):
        if c > 0:
            prepare(c)
        far_own(c).start()
        mate_own(c).start()

        @pl.when(straight)
        def _():
            across_own(c).start()

    @pl.when(turned)
    def _():
        for c in range(CHUNKS):
            got(outer, 1, c)
            across_turn(c).start()

    temper = jnp.exp(jnp.full((1, half), log_temp[0], jnp.float32))
    slope = 0.5 * temper
    shift = jnp.full((1, half), 0.5 * bias[0], jnp.float32)
    grads[...] = jnp.zeros_like(grads)
    loss_acc[...] = jnp.zeros_like(loss_acc)

    def step(side, block, h, diagonal=False):
        @pl.loop(0, HALVES)
        def _(m):
            part = pl.ds(pl.multiple_of(m * half, half), half)
            own = low[side, part, :]
            dots = lax.dot_general(own, block, NT, preferred_element_type=jnp.float32)
            turn = jnp.tanh(dots * slope + shift)
            weights = slope + slope * turn
            other_side = 0.5 - 0.5 * turn
            if diagonal:
                row = lax.broadcasted_iota(jnp.int32, (half, half), 0)
                column = lax.broadcasted_iota(jnp.int32, (half, half), 1)
                positive = row + m * half == column + h * half
                weights = jnp.where(positive, slope * turn - slope, weights)
                other_side = jnp.where(positive, 0.5 + 0.5 * turn, other_side)
            product = other_side[:, :128]
            for at in range(128, half, 128):
                product = product * other_side[:, at : at + 128]
            loss_acc[side, part, :] -= jnp.log(product)
            grads[side, part, :] += jnp.dot(
                weights.astype(jnp.bfloat16), block, preferred_element_type=jnp.float32
            )

    def own_step(side):
        for h in range(HALVES):
            step(side, low[1 - side, pl.ds(h * half, half), :], h, True)

    def came_step(side, j, h):
        step(side, came[side, j, pl.ds(h * half, half), :], h)

    per = CHUNKS // HALVES

    def early(c):
        got(outer, 0, c)
        far_pass(c).start()
        got(inner, 1, c)

        @pl.when(straight)
        def _():
            across_turn(c).start()
            got(outer, 1, c)

        @pl.when(turned)
        def _():
            across_own(c).start()

    def late(c):
        got(inner, 0, c)
        mate_pass(c).start()

    own_step(0)
    early(0)
    own_step(1)
    early(1)
    came_step(outer, 1, 0)
    came_step(inner, 1, 0)
    early(2)
    came_step(outer, 0, 0)
    early(3)
    came_step(outer, 1, 1)
    came_step(inner, 1, 1)
    came_step(outer, 0, 1)
    for h in range(HALVES):
        pieces = range(h * per, (h + 1) * per)
        for c in pieces:
            late(c)
        came_step(inner, 0, h)
        for c in pieces:
            got(inner, 2, c)
        came_step(inner, 2, h)
        for c in pieces:
            got(outer, 2, c)
        came_step(outer, 2, h)

    for side in range(2):

        @pl.loop(0, CHUNKS)
        def _(c):
            part = pl.ds(pl.multiple_of(c * piece, piece), piece)
            values = held[side, part, :].astype(jnp.float32)
            scale = row_scale(values)
            unit = values * scale
            grad = grads[side, part, :]
            grads[side, part, :] = scale * (
                grad - unit * jnp.sum(unit * grad, axis=-1, keepdims=True)
            )

    for at in range(rows // 128):
        part = loss_acc[0, at * 128 : (at + 1) * 128, :]
        loss_out[at : at + 1, :] = jnp.sum(part.T, axis=0, keepdims=True)

    for c in range(CHUNKS):
        for sent in (far_own, mate_own, far_pass, mate_pass, across_own, across_turn):
            sent(c).wait_send()


def body(blocks, image_emb, text_emb, log_temp, bias):
    rows, width = image_emb.shape
    vmem = pl.BlockSpec(memory_space=pltpu.VMEM)
    hbm = pl.BlockSpec(memory_space=pltpu.HBM)
    smem = pl.BlockSpec(memory_space=pltpu.SMEM)
    losses, grads = pl.pallas_call(
        functools.partial(kernel, blocks),
        out_shape=(
            jax.ShapeDtypeStruct((rows // 128, 128), jnp.float32),
            jax.ShapeDtypeStruct((2, rows, width), jnp.float32),
        ),
        in_specs=[smem, smem, hbm, hbm],
        out_specs=(vmem, vmem),
        scratch_shapes=[
            pltpu.VMEM((2, rows, width), jnp.bfloat16),
            pltpu.VMEM((2, rows, width), jnp.bfloat16),
            pltpu.VMEM((2, 3, rows, width), jnp.bfloat16),
            pltpu.VMEM((2, rows, 128), jnp.float32),
            pltpu.SemaphoreType.DMA((2, CHUNKS)),
            pltpu.SemaphoreType.DMA((6, CHUNKS)),
            pltpu.SemaphoreType.DMA((2, 3, CHUNKS)),
        ],
        compiler_params=pltpu.CompilerParams(
            collective_id=0, has_side_effects=True, vmem_limit_bytes=44 * 1024 * 1024
        ),
        cost_estimate=pl.CostEstimate(
            flops=32 * rows * rows * width,
            bytes_accessed=12 * rows * width,
            transcendentals=14 * rows * rows,
        ),
    )(log_temp.reshape(1), bias.reshape(1), image_emb, text_emb)
    return losses.reshape(rows), grads[0], grads[1]


def solution(mesh):
    if mesh.shape["rep"] != 2 or mesh.shape["blk"] % 2:
        raise ValueError("mesh")
    return jax.shard_map(
        functools.partial(body, mesh.shape["blk"]),
        mesh=mesh,
        in_specs=(P(("blk", "rep"), None), P(("blk", "rep"), None), P(), P()),
        out_specs=(P(("blk", "rep")), P(("blk", "rep"), None), P(("blk", "rep"), None)),
        check_vma=False,
    )
```

time: 310 us -> 75.3 us (0.24)
  waiting for transfers between devices: 274 us -> 0 us
  Pallas kernels: 0 us -> 67.6 us
  matrix products: 14.4 us -> 0 us
  other arithmetic: 8.7 us -> 0 us
  starting transfers between devices: 7.46 us -> 0 us
  local copies, waits for them, and re-layouts: 0.01 us -> 5.6 us
    ppermute x7 -> x0, waiting for transfers between devices: 274 us -> none  [shifted(): return lax.ppermute(x, axis, [(i, (i + by) % count) for i in range(count)])]
    pallas_call x0 -> x1, Pallas kernels: none -> 67.6 us  [body(): pl.pallas_call(functools.partial(kernel, blocks), out_shape=(jax.ShapeDty...]
    dot_general x12 -> x0, matrix products: 14.4 us -> none  [the longest x4 6.05 us: block_weights(): lax.dot_general(image_low, partner, (((1,), (1,)), ((), ())), preferred_e...]
    ppermute x7 -> x0, starting transfers between devices: 7.46 us -> none  [shifted(): return lax.ppermute(x, axis, [(i, (i + by) % count) for i in range(count)])]
    mul x2 -> x0, other arithmetic: 3.75 us -> none  [unit_backward(): scale * (grad_unit - unit * jnp.sum(unit * grad_unit, axis=-1, keepdims=T...]
    unnamed x4 -> x5, local copies, waits for them, and re-layouts: 0.01 us -> 3.11 us
  transfers between devices with their start and end apart: 7 -> 0, of which waited for: 4 -> 0; matrix products, arithmetic and copies ran while one was open for 4% -> 0% of each run, Pallas kernels for 0% -> 0%
where the time goes in v3:
time: 75.3 us; the launch traced here: 75.1 us
  Pallas kernels  67.6 us (90%)
  local copies, waits for them, and re-layouts  5.6 us (7%)
  between operations  1.94 us (3%)
    pallas_call x1, Pallas kernels, body(): pl.pallas_call(functools.partial(kernel, blocks), out_shape=(jax.ShapeDty...  67.6 us
    unnamed x5, local copies, waits for them, and re-layouts  3.11 us
    squeeze x1, local copies, waits for them, and re-layouts, body(): return (losses.reshape(rows), grads[0], grads[1])  2.49 us

profile of v3, /device:TPU:1, one launch (start us, length us, event | category | flops | bytes accessed | tf_op | source)
XLA Modules:
  0.0 75.1 jit_solution(4217206530236591980)
XLA Ops:
  1.9 0.0 copy-start
  1.9 1.3 %copy-done = bf16[512,1152]{1,0:T(8,128)(2,1)S(1)} copy-done((bf16[512,1152]{1,0:T(8,128)(2,1)S(1)}, bf16[512,1152]{1,0:T(8,128)(2,1)}, u32[]{:S(2)}) %copy-start) | copy-done | bytes 1179672
  3.2 0.0 copy-start.1
  3.2 1.3 %copy-done.1 = bf16[512,1152]{1,0:T(8,128)(2,1)S(1)} copy-done((bf16[512,1152]{1,0:T(8,128)(2,1)S(1)}, bf16[512,1152]{1,0:T(8,128)(2,1)}, u32[]{:S(2)}) %copy-start.1) | copy-done | bytes 1179672
  4.5 67.6 %shard_map.67 = (f32[4,128]{1,0:T(4,128)S(1)}, f32[2,512,1152]{2,1,0:T(8,128)S(1)}) custom-call(f32[1]{0:T(128)} %bitcast.7.log_temp, f32[1]{0:T(128)} %bitcast.8.bias, bf16[512,1152]{1,0:T(8,128)(2,1)S(1)} %copy-done, bf16[512,1152]{1,0:T(8,128)(2,1)S(1)} %copy-done.1), custom_call_target="tpu_custom_call" | custom-call | flops 9663676416 | bytes 7077888 | tf_op jit(solution)/shard_map/pallas_call | solution.py:226
  72.1 2.5 %slice_bitcast_fusion = (f32[512,1152]{1,0:T(8,128)}, f32[512,1152]{1,0:T(8,128)}) fusion(f32[2,512,1152]{2,1,0:T(8,128)S(1)} %get-tuple-element.6), kind=kLoop, calls=%fused_computation | loop fusion | bytes 9437184 | tf_op jit(solution)/shard_map/squeeze | solution.py:252
  74.6 0.6 copy.10
Async XLA Ops:
  1.9 1.3 %copy-start = (bf16[512,1152]{1,0:T(8,128)(2,1)S(1)}, bf16[512,1152]{1,0:T(8,128)(2,1)}, u32[]{:S(2)}) copy-start(bf16[512,1152]{1,0:T(8,128)(2,1)} %image_emb.1) | copy-start | bytes 3538948
  3.2 1.3 %copy-start.1 = (bf16[512,1152]{1,0:T(8,128)(2,1)S(1)}, bf16[512,1152]{1,0:T(8,128)(2,1)}, u32[]{:S(2)}) copy-start(bf16[512,1152]{1,0:T(8,128)(2,1)} %text_emb.1) | copy-start | bytes 3538948

commit v4 on v3

--- a/solution.py
+++ b/solution.py
@@ -9,7 +9,8 @@
 
 EPSILON = 1e-06
 MESH = pl.DeviceIdType.MESH
-CHUNKS = 4
+CHUNKS = 8
+PIECES = 8
 HALVES = 2
 NT = (((1,), (1,)), ((), ()))
 
@@ -24,12 +25,11 @@
     bias,
     image_emb,
     text_emb,
-    loss_out,
+    loss_acc,
     grads,
     held,
     low,
     came,
-    loss_acc,
     fetch_sem,
     send_sem,
     came_sem,
@@ -154,7 +154,11 @@
 
     per = CHUNKS // HALVES
 
-    def early(c):
+    def early(quarter):
+        for c in range(quarter * CHUNKS // 4, (quarter + 1) * CHUNKS // 4):
+            early_chunk(c)
+
+    def early_chunk(c):
         got(outer, 0, c)
         far_pass(c).start()
         got(inner, 1, c)
@@ -196,26 +200,42 @@
             got(outer, 2, c)
         came_step(outer, 2, h)
 
-    for side in range(2):
-
-        @pl.loop(0, CHUNKS)
-        def _(c):
-            part = pl.ds(pl.multiple_of(c * piece, piece), piece)
-            values = held[side, part, :].astype(jnp.float32)
+    for c in range(CHUNKS):
+        for sent in (far_own, mate_own, far_pass, mate_pass, across_own, across_turn):
+            sent(c).wait_send()
+
+
+def finish(loss_acc, grads, image_emb, text_emb, loss_out, image_out, text_out, loss, done, sem, loss_sem):
+    rows = grads.shape[1]
+    piece = rows // PIECES
+
+    def store(side, c):
+        part = pl.ds(c * piece, piece)
+        out = text_out if side else image_out
+        return pltpu.make_async_copy(done.at[side, part, :], out.at[part, :], sem.at[side, c])
+
+    def store_loss():
+        return pltpu.make_async_copy(loss, loss_out, loss_sem)
+
+    for c in range(PIECES):
+        part = pl.ds(c * piece, piece)
+        for side in range(2):
+            emb = text_emb if side else image_emb
+            values = emb[part, :].astype(jnp.float32)
             scale = row_scale(values)
             unit = values * scale
             grad = grads[side, part, :]
-            grads[side, part, :] = scale * (
-                grad - unit * jnp.sum(unit * grad, axis=-1, keepdims=True)
-            )
-
+            along = jnp.sum(unit * grad, axis=-1, keepdims=True)
+            done[side, part, :] = scale * (grad - unit * along)
+            store(side, c).start()
     for at in range(rows // 128):
         part = loss_acc[0, at * 128 : (at + 1) * 128, :]
-        loss_out[at : at + 1, :] = jnp.sum(part.T, axis=0, keepdims=True)
-
-    for c in range(CHUNKS):
-        for sent in (far_own, mate_own, far_pass, mate_pass, across_own, across_turn):
-            sent(c).wait_send()
+        loss[at : at + 1, :] = jnp.sum(part.T, axis=0, keepdims=True)
+    store_loss().start()
+    for c in range(PIECES):
+        for side in range(2):
+            store(side, c).wait()
+    store_loss().wait()
 
 
 def body(blocks, image_emb, text_emb, log_temp, bias):
@@ -223,10 +243,10 @@
     vmem = pl.BlockSpec(memory_space=pltpu.VMEM)
     hbm = pl.BlockSpec(memory_space=pltpu.HBM)
     smem = pl.BlockSpec(memory_space=pltpu.SMEM)
-    losses, grads = pl.pallas_call(
+    loss_acc, grads = pl.pallas_call(
         functools.partial(kernel, blocks),
         out_shape=(
-            jax.ShapeDtypeStruct((rows // 128, 128), jnp.float32),
+            jax.ShapeDtypeStruct((2, rows, 128), jnp.float32),
             jax.ShapeDtypeStruct((2, rows, width), jnp.float32),
         ),
         in_specs=[smem, smem, hbm, hbm],
@@ -235,7 +255,6 @@
             pltpu.VMEM((2, rows, width), jnp.bfloat16),
             pltpu.VMEM((2, rows, width), jnp.bfloat16),
             pltpu.VMEM((2, 3, rows, width), jnp.bfloat16),
-            pltpu.VMEM((2, rows, 128), jnp.float32),
             pltpu.SemaphoreType.DMA((2, CHUNKS)),
             pltpu.SemaphoreType.DMA((6, CHUNKS)),
             pltpu.SemaphoreType.DMA((2, 3, CHUNKS)),
@@ -249,7 +268,27 @@
             transcendentals=14 * rows * rows,
         ),
     )(log_temp.reshape(1), bias.reshape(1), image_emb, text_emb)
-    return losses.reshape(rows), grads[0], grads[1]
+    losses, grad_image, grad_text = pl.pallas_call(
+        finish,
+        out_shape=(
+            jax.ShapeDtypeStruct((rows // 128, 128), jnp.float32),
+            jax.ShapeDtypeStruct((rows, width), jnp.float32),
+            jax.ShapeDtypeStruct((rows, width), jnp.float32),
+        ),
+        in_specs=[vmem] * 4,
+        out_specs=(hbm, hbm, hbm),
+        scratch_shapes=[
+            pltpu.VMEM((rows // 128, 128), jnp.float32),
+            pltpu.VMEM((2, rows, width), jnp.float32),
+            pltpu.SemaphoreType.DMA((2, PIECES)),
+            pltpu.SemaphoreType.DMA,
+        ],
+        compiler_params=pltpu.CompilerParams(vmem_limit_bytes=20 * 1024 * 1024),
+        cost_estimate=pl.CostEstimate(
+            flops=16 * rows * width, bytes_accessed=8 * rows * width, transcendentals=2 * rows
+        ),
+    )(loss_acc, grads, image_emb, text_emb)
+    return losses.reshape(rows), grad_image, grad_text
 
 
 def solution(mesh):

time: 75.3 us -> 75.9 us (level)
  Pallas kernels: 67.6 us -> 71.2 us
  local copies, waits for them, and re-layouts: 5.6 us -> 2.53 us
    pallas_call x0 -> x1, Pallas kernels: none -> 2.77 us  [body(): pl.pallas_call(finish, out_shape=(jax.ShapeDtypeStruct((rows // 128, 128)...]
    squeeze x1 -> x0, local copies, waits for them, and re-layouts: 2.49 us -> none  [body(): return (losses.reshape(rows), grads[0], grads[1])]
    pallas_call x1, Pallas kernels: 67.6 us -> 68.4 us  [body(): pl.pallas_call(functools.partial(kernel, blocks), out_shape=(jax.ShapeDty...]
    unnamed x5 -> x4, local copies, waits for them, and re-layouts: 3.11 us -> 2.53 us
where the time goes in v4:
time: 75.9 us; the launch traced here: 75.7 us
  Pallas kernels  71.2 us (94%)
  local copies, waits for them, and re-layouts  2.53 us (3%)
  between operations  1.94 us (3%)
    pallas_call x1, Pallas kernels, body(): pl.pallas_call(functools.partial(kernel, blocks), out_shape=(jax.ShapeDty...  68.4 us
    pallas_call x1, Pallas kernels, body(): pl.pallas_call(finish, out_shape=(jax.ShapeDtypeStruct((rows // 128, 128)...  2.77 us
    unnamed x4, local copies, waits for them, and re-layouts  2.53 us

profile of v4, /device:TPU:1, one launch (start us, length us, event | category | flops | bytes accessed | tf_op | source)
XLA Modules:
  0.0 75.7 jit_solution(17595607001188941999)
XLA Ops:
  1.9 0.0 copy-start
  1.9 1.3 %copy-done = bf16[512,1152]{1,0:T(8,128)(2,1)S(1)} copy-done((bf16[512,1152]{1,0:T(8,128)(2,1)S(1)}, bf16[512,1152]{1,0:T(8,128)(2,1)}, u32[]{:S(2)}) %copy-start) | copy-done | bytes 1179672
  3.2 0.0 copy-start.1
  3.2 1.3 %copy-done.1 = bf16[512,1152]{1,0:T(8,128)(2,1)S(1)} copy-done((bf16[512,1152]{1,0:T(8,128)(2,1)S(1)}, bf16[512,1152]{1,0:T(8,128)(2,1)}, u32[]{:S(2)}) %copy-start.1) | copy-done | bytes 1179672
  4.5 68.4 %shard_map.67 = (f32[2,512,128]{2,1,0:T(8,128)S(1)}, f32[2,512,1152]{2,1,0:T(8,128)S(1)}) custom-call(f32[1]{0:T(128)} %bitcast.3.log_temp, f32[1]{0:T(128)} %bitcast.4.bias, bf16[512,1152]{1,0:T(8,128)(2,1)S(1)} %copy-done, bf16[512,1152]{1,0:T(8,128)(2,1)S(1)} %copy-done.1), custom_call_target="tpu_custom_call" | custom-call | flops 9663676416 | bytes 7077888 | tf_op jit(solution)/shard_map/pallas_call | solution.py:246
  72.9 2.8 %shard_map.68 = (f32[4,128]{1,0:T(4,128)}, f32[512,1152]{1,0:T(8,128)}, f32[512,1152]{1,0:T(8,128)}) custom-call(f32[2,512,128]{2,1,0:T(8,128)S(1)} %get-tuple-element.8.loss_acc, f32[2,512,1152]{2,1,0:T(8,128)S(1)} %get-tuple-element.9.grads, bf16[512,1152]{1,0:T(8,128)(2,1)S(1)} %copy-done, bf16[512,1152]{1,0:T(8,128)(2,1)S(1)} %copy-done.1), custom_call_target="tpu_custom_call" | custom-call | flops 9437184 | bytes 4718592 | tf_op jit(solution)/shard_map/pallas_call | solution.py:271
Async XLA Ops:
  1.9 1.3 %copy-start = (bf16[512,1152]{1,0:T(8,128)(2,1)S(1)}, bf16[512,1152]{1,0:T(8,128)(2,1)}, u32[]{:S(2)}) copy-start(bf16[512,1152]{1,0:T(8,128)(2,1)} %image_emb.3) | copy-start | bytes 3538948
  3.2 1.3 %copy-start.1 = (bf16[512,1152]{1,0:T(8,128)(2,1)S(1)}, bf16[512,1152]{1,0:T(8,128)(2,1)}, u32[]{:S(2)}) copy-start(bf16[512,1152]{1,0:T(8,128)(2,1)} %text_emb.3) | copy-start | bytes 3538948

commit v5 on v4

--- a/solution.py
+++ b/solution.py
@@ -9,7 +9,7 @@
 
 EPSILON = 1e-06
 MESH = pl.DeviceIdType.MESH
-CHUNKS = 8
+CHUNKS = 4
 PIECES = 8
 HALVES = 2
 NT = (((1,), (1,)), ((), ()))
@@ -123,27 +123,23 @@
     loss_acc[...] = jnp.zeros_like(loss_acc)
 
     def step(side, block, h, diagonal=False):
-        @pl.loop(0, HALVES)
-        def _(m):
-            part = pl.ds(pl.multiple_of(m * half, half), half)
-            own = low[side, part, :]
-            dots = lax.dot_general(own, block, NT, preferred_element_type=jnp.float32)
-            turn = jnp.tanh(dots * slope + shift)
-            weights = slope + slope * turn
-            other_side = 0.5 - 0.5 * turn
-            if diagonal:
-                row = lax.broadcasted_iota(jnp.int32, (half, half), 0)
-                column = lax.broadcasted_iota(jnp.int32, (half, half), 1)
-                positive = row + m * half == column + h * half
-                weights = jnp.where(positive, slope * turn - slope, weights)
-                other_side = jnp.where(positive, 0.5 + 0.5 * turn, other_side)
-            product = other_side[:, :128]
-            for at in range(128, half, 128):
-                product = product * other_side[:, at : at + 128]
-            loss_acc[side, part, :] -= jnp.log(product)
-            grads[side, part, :] += jnp.dot(
-                weights.astype(jnp.bfloat16), block, preferred_element_type=jnp.float32
-            )
+        dots = lax.dot_general(low[side], block, NT, preferred_element_type=jnp.float32)
+        turn = jnp.tanh(dots * slope + shift)
+        weights = slope + slope * turn
+        other_side = 1.0 - turn
+        if diagonal:
+            row = lax.broadcasted_iota(jnp.int32, (rows, half), 0)
+            column = lax.broadcasted_iota(jnp.int32, (rows, half), 1)
+            positive = row == column + h * half
+            weights = jnp.where(positive, slope * turn - slope, weights)
+            other_side = jnp.where(positive, 1.0 + turn, other_side)
+        product = 1.0
+        for at in range(0, half, 128):
+            product = product * (0.5 * other_side[:, at : at + 128])
+        loss_acc[side] -= jnp.log(product)
+        grads[side] += jnp.dot(
+            weights.astype(jnp.bfloat16), block, preferred_element_type=jnp.float32
+        )
 
     def own_step(side):
         for h in range(HALVES):
@@ -185,20 +181,25 @@
     early(2)
     came_step(outer, 0, 0)
     early(3)
+    for c in range(per):
+        late(c)
     came_step(outer, 1, 1)
     came_step(inner, 1, 1)
     came_step(outer, 0, 1)
-    for h in range(HALVES):
-        pieces = range(h * per, (h + 1) * per)
-        for c in pieces:
-            late(c)
-        came_step(inner, 0, h)
-        for c in pieces:
-            got(inner, 2, c)
-        came_step(inner, 2, h)
-        for c in pieces:
-            got(outer, 2, c)
-        came_step(outer, 2, h)
+    came_step(inner, 0, 0)
+    for c in range(per, CHUNKS):
+        late(c)
+
+    def last_step(side, h):
+        for c in range(h * per, (h + 1) * per):
+            got(side, 2, c)
+        came_step(side, 2, h)
+
+    last_step(inner, 0)
+    last_step(outer, 0)
+    came_step(inner, 0, 1)
+    last_step(inner, 1)
+    last_step(outer, 1)
 
     for c in range(CHUNKS):
         for sent in (far_own, mate_own, far_pass, mate_pass, across_own, across_turn):

time: 75.9 us -> 74.2 us (0.978)
  Pallas kernels: 71.2 us -> 69.4 us
    pallas_call x1, Pallas kernels: 68.4 us -> 66.6 us  [body(): pl.pallas_call(functools.partial(kernel, blocks), out_shape=(jax.ShapeDty...]
where the time goes in v5:
time: 74.2 us; the launch traced here: 74 us
  Pallas kernels  69.4 us (94%)
  local copies, waits for them, and re-layouts  2.53 us (3%)
  between operations  2.1 us (3%)
    pallas_call x1, Pallas kernels, body(): pl.pallas_call(functools.partial(kernel, blocks), out_shape=(jax.ShapeDty...  66.6 us
    pallas_call x1, Pallas kernels, body(): pl.pallas_call(finish, out_shape=(jax.ShapeDtypeStruct((rows // 128, 128)...  2.77 us
    unnamed x4, local copies, waits for them, and re-layouts  2.53 us

profile of v5, /device:TPU:1, one launch (start us, length us, event | category | flops | bytes accessed | tf_op | source)
XLA Modules:
  0.0 74.0 jit_solution(10089240608874786919)
XLA Ops:
  1.9 0.0 copy-start
  1.9 1.3 %copy-done = bf16[512,1152]{1,0:T(8,128)(2,1)S(1)} copy-done((bf16[512,1152]{1,0:T(8,128)(2,1)S(1)}, bf16[512,1152]{1,0:T(8,128)(2,1)}, u32[]{:S(2)}) %copy-start) | copy-done | bytes 1179672
  3.2 0.0 copy-start.1
  3.2 1.3 %copy-done.1 = bf16[512,1152]{1,0:T(8,128)(2,1)S(1)} copy-done((bf16[512,1152]{1,0:T(8,128)(2,1)S(1)}, bf16[512,1152]{1,0:T(8,128)(2,1)}, u32[]{:S(2)}) %copy-start.1) | copy-done | bytes 1179672
  4.5 66.6 %shard_map.67 = (f32[2,512,128]{2,1,0:T(8,128)S(1)}, f32[2,512,1152]{2,1,0:T(8,128)S(1)}) custom-call(f32[1]{0:T(128)} %bitcast.3.log_temp, f32[1]{0:T(128)} %bitcast.4.bias, bf16[512,1152]{1,0:T(8,128)(2,1)S(1)} %copy-done, bf16[512,1152]{1,0:T(8,128)(2,1)S(1)} %copy-done.1), custom_call_target="tpu_custom_call" | custom-call | flops 9663676416 | bytes 7077888 | tf_op jit(solution)/shard_map/pallas_call | solution.py:247
  71.1 2.8 %shard_map.68 = (f32[4,128]{1,0:T(4,128)}, f32[512,1152]{1,0:T(8,128)}, f32[512,1152]{1,0:T(8,128)}) custom-call(f32[2,512,128]{2,1,0:T(8,128)S(1)} %get-tuple-element.8.loss_acc, f32[2,512,1152]{2,1,0:T(8,128)S(1)} %get-tuple-element.9.grads, bf16[512,1152]{1,0:T(8,128)(2,1)S(1)} %copy-done, bf16[512,1152]{1,0:T(8,128)(2,1)S(1)} %copy-done.1), custom_call_target="tpu_custom_call" | custom-call | flops 9437184 | bytes 4718592 | tf_op jit(solution)/shard_map/pallas_call | solution.py:272
Async XLA Ops:
  1.9 1.3 %copy-start = (bf16[512,1152]{1,0:T(8,128)(2,1)S(1)}, bf16[512,1152]{1,0:T(8,128)(2,1)}, u32[]{:S(2)}) copy-start(bf16[512,1152]{1,0:T(8,128)(2,1)} %image_emb.3) | copy-start | bytes 3538948
  3.2 1.3 %copy-start.1 = (bf16[512,1152]{1,0:T(8,128)(2,1)S(1)}, bf16[512,1152]{1,0:T(8,128)(2,1)}, u32[]{:S(2)}) copy-start(bf16[512,1152]{1,0:T(8,128)(2,1)} %text_emb.3) | copy-start | bytes 3538948

commit v6 on v5

--- a/solution.py
+++ b/solution.py
@@ -150,13 +150,7 @@
 
     per = CHUNKS // HALVES
 
-    def early(quarter):
-        for c in range(quarter * CHUNKS // 4, (quarter + 1) * CHUNKS // 4):
-            early_chunk(c)
-
-    def early_chunk(c):
-        got(outer, 0, c)
-        far_pass(c).start()
+    def early(c):
         got(inner, 1, c)
 
         @pl.when(straight)
@@ -164,9 +158,9 @@
             across_turn(c).start()
             got(outer, 1, c)
 
-        @pl.when(turned)
-        def _():
-            across_own(c).start()
+    def forward(c):
+        got(outer, 0, c)
+        far_pass(c).start()
 
     def late(c):
         got(inner, 0, c)
@@ -179,24 +173,34 @@
     came_step(outer, 1, 0)
     came_step(inner, 1, 0)
     early(2)
+    early(3)
+
+    @pl.when(turned)
+    def _():
+        for c in range(CHUNKS):
+            across_own(c).start()
+
+    forward(0)
+    forward(1)
+    came_step(outer, 1, 1)
+    forward(2)
+    came_step(inner, 1, 1)
+    forward(3)
     came_step(outer, 0, 0)
-    early(3)
-    for c in range(per):
-        late(c)
-    came_step(outer, 1, 1)
-    came_step(inner, 1, 1)
     came_step(outer, 0, 1)
+    late(0)
+    late(1)
     came_step(inner, 0, 0)
-    for c in range(per, CHUNKS):
-        late(c)
 
     def last_step(side, h):
         for c in range(h * per, (h + 1) * per):
             got(side, 2, c)
         came_step(side, 2, h)
 
+    last_step(outer, 0)
+    late(2)
+    late(3)
     last_step(inner, 0)
-    last_step(outer, 0)
     came_step(inner, 0, 1)
     last_step(inner, 1)
     last_step(outer, 1)

time: 74.2 us -> 72.6 us (0.978)
  Pallas kernels: 69.4 us -> 67.7 us
    pallas_call x1, Pallas kernels: 66.6 us -> 65 us  [body(): pl.pallas_call(functools.partial(kernel, blocks), out_shape=(jax.ShapeDty...]
where the time goes in v6:
time: 72.6 us; the launch traced here: 72.4 us
  Pallas kernels  67.7 us (93%)
  local copies, waits for them, and re-layouts  2.53 us (3%)
  between operations  2.1 us (3%)
    pallas_call x1, Pallas kernels, body(): pl.pallas_call(functools.partial(kernel, blocks), out_shape=(jax.ShapeDty...  65 us
    pallas_call x1, Pallas kernels, body(): pl.pallas_call(finish, out_shape=(jax.ShapeDtypeStruct((rows // 128, 128)...  2.77 us
    unnamed x4, local copies, waits for them, and re-layouts  2.53 us

profile of v6, /device:TPU:1, one launch (start us, length us, event | category | flops | bytes accessed | tf_op | source)
XLA Modules:
  0.0 72.4 jit_solution(8899890916737316307)
XLA Ops:
  1.9 0.0 copy-start
  1.9 1.3 %copy-done = bf16[512,1152]{1,0:T(8,128)(2,1)S(1)} copy-done((bf16[512,1152]{1,0:T(8,128)(2,1)S(1)}, bf16[512,1152]{1,0:T(8,128)(2,1)}, u32[]{:S(2)}) %copy-start) | copy-done | bytes 1179672
  3.2 0.0 copy-start.1
  3.2 1.3 %copy-done.1 = bf16[512,1152]{1,0:T(8,128)(2,1)S(1)} copy-done((bf16[512,1152]{1,0:T(8,128)(2,1)S(1)}, bf16[512,1152]{1,0:T(8,128)(2,1)}, u32[]{:S(2)}) %copy-start.1) | copy-done | bytes 1179672
  4.5 65.0 %shard_map.67 = (f32[2,512,128]{2,1,0:T(8,128)S(1)}, f32[2,512,1152]{2,1,0:T(8,128)S(1)}) custom-call(f32[1]{0:T(128)} %bitcast.3.log_temp, f32[1]{0:T(128)} %bitcast.4.bias, bf16[512,1152]{1,0:T(8,128)(2,1)S(1)} %copy-done, bf16[512,1152]{1,0:T(8,128)(2,1)S(1)} %copy-done.1), custom_call_target="tpu_custom_call" | custom-call | flops 9663676416 | bytes 7077888 | tf_op jit(solution)/shard_map/pallas_call | solution.py:251
  69.4 2.8 %shard_map.68 = (f32[4,128]{1,0:T(4,128)}, f32[512,1152]{1,0:T(8,128)}, f32[512,1152]{1,0:T(8,128)}) custom-call(f32[2,512,128]{2,1,0:T(8,128)S(1)} %get-tuple-element.8.loss_acc, f32[2,512,1152]{2,1,0:T(8,128)S(1)} %get-tuple-element.9.grads, bf16[512,1152]{1,0:T(8,128)(2,1)S(1)} %copy-done, bf16[512,1152]{1,0:T(8,128)(2,1)S(1)} %copy-done.1), custom_call_target="tpu_custom_call" | custom-call | flops 9437184 | bytes 4718592 | tf_op jit(solution)/shard_map/pallas_call | solution.py:276
Async XLA Ops:
  1.9 1.3 %copy-start = (bf16[512,1152]{1,0:T(8,128)(2,1)S(1)}, bf16[512,1152]{1,0:T(8,128)(2,1)}, u32[]{:S(2)}) copy-start(bf16[512,1152]{1,0:T(8,128)(2,1)} %image_emb.3) | copy-start | bytes 3538948
  3.2 1.3 %copy-start.1 = (bf16[512,1152]{1,0:T(8,128)(2,1)S(1)}, bf16[512,1152]{1,0:T(8,128)(2,1)}, u32[]{:S(2)}) copy-start(bf16[512,1152]{1,0:T(8,128)(2,1)} %text_emb.3) | copy-start | bytes 3538948

commit v7 on v6

--- a/solution.py
+++ b/solution.py
@@ -27,10 +27,8 @@
     text_emb,
     loss_acc,
     grads,
-    held,
     low,
     came,
-    fetch_sem,
     send_sem,
     came_sem,
 ):
@@ -48,23 +46,14 @@
     def chunk(c):
         return pl.ds(c * piece, piece)
 
-    def fetch(side, c):
-        emb = text_emb if side else image_emb
-        return pltpu.make_async_copy(
-            emb.at[chunk(c), :], held.at[side, chunk(c), :], fetch_sem.at[side, c]
-        )
-
-    for c in range(CHUNKS):
-        fetch(0, c).start()
-        fetch(1, c).start()
     barrier = pltpu.get_barrier_semaphore()
     for other in (mate, far, across):
         pl.semaphore_signal(barrier, inc=1, device_id=other, device_id_type=MESH)
 
     def prepare(c):
         for side in range(2):
-            fetch(side, c).wait()
-            values = held[side, chunk(c), :].astype(jnp.float32)
+            emb = text_emb if side else image_emb
+            values = emb[chunk(c), :].astype(jnp.float32)
             low[side, chunk(c), :] = (values * row_scale(values)).astype(jnp.bfloat16)
 
     def copy(kind, c, src, side, j, to):
@@ -198,9 +187,9 @@
         came_step(side, 2, h)
 
     last_step(outer, 0)
+    last_step(inner, 0)
     late(2)
     late(3)
-    last_step(inner, 0)
     came_step(inner, 0, 1)
     last_step(inner, 1)
     last_step(outer, 1)
@@ -254,13 +243,11 @@
             jax.ShapeDtypeStruct((2, rows, 128), jnp.float32),
             jax.ShapeDtypeStruct((2, rows, width), jnp.float32),
         ),
-        in_specs=[smem, smem, hbm, hbm],
+        in_specs=[smem, smem, vmem, vmem],
         out_specs=(vmem, vmem),
         scratch_shapes=[
             pltpu.VMEM((2, rows, width), jnp.bfloat16),
-            pltpu.VMEM((2, rows, width), jnp.bfloat16),
             pltpu.VMEM((2, 3, rows, width), jnp.bfloat16),
-            pltpu.SemaphoreType.DMA((2, CHUNKS)),
             pltpu.SemaphoreType.DMA((6, CHUNKS)),
             pltpu.SemaphoreType.DMA((2, 3, CHUNKS)),
         ],

time: 72.6 us -> 71.3 us (0.982)
  Pallas kernels: 67.7 us -> 66.4 us
    pallas_call x1, Pallas kernels: 65 us -> 63.7 us  [body(): pl.pallas_call(functools.partial(kernel, blocks), out_shape=(jax.ShapeDty...]
where the time goes in v7:
time: 71.3 us; the launch traced here: 71.1 us
  Pallas kernels  66.4 us (93%)
  local copies, waits for them, and re-layouts  2.53 us (4%)
  between operations  2.1 us (3%)
    pallas_call x1, Pallas kernels, body(): pl.pallas_call(functools.partial(kernel, blocks), out_shape=(jax.ShapeDty...  63.7 us
    pallas_call x1, Pallas kernels, body(): pl.pallas_call(finish, out_shape=(jax.ShapeDtypeStruct((rows // 128, 128)...  2.77 us
    unnamed x4, local copies, waits for them, and re-layouts  2.53 us

profile of v7, /device:TPU:1, one launch (start us, length us, event | category | flops | bytes accessed | tf_op | source)
XLA Modules:
  0.0 71.1 jit_solution(9182808303176732518)
XLA Ops:
  1.9 0.0 copy-start
  1.9 1.3 %copy-done = bf16[512,1152]{1,0:T(8,128)(2,1)S(1)} copy-done((bf16[512,1152]{1,0:T(8,128)(2,1)S(1)}, bf16[512,1152]{1,0:T(8,128)(2,1)}, u32[]{:S(2)}) %copy-start) | copy-done | bytes 1179672
  3.2 0.0 copy-start.1
  3.2 1.3 %copy-done.1 = bf16[512,1152]{1,0:T(8,128)(2,1)S(1)} copy-done((bf16[512,1152]{1,0:T(8,128)(2,1)S(1)}, bf16[512,1152]{1,0:T(8,128)(2,1)}, u32[]{:S(2)}) %copy-start.1) | copy-done | bytes 1179672
  4.5 63.7 %shard_map.67 = (f32[2,512,128]{2,1,0:T(8,128)S(1)}, f32[2,512,1152]{2,1,0:T(8,128)S(1)}) custom-call(f32[1]{0:T(128)} %bitcast.3.log_temp, f32[1]{0:T(128)} %bitcast.4.bias, bf16[512,1152]{1,0:T(8,128)(2,1)S(1)} %copy-done, bf16[512,1152]{1,0:T(8,128)(2,1)S(1)} %copy-done.1), custom_call_target="tpu_custom_call" | custom-call | flops 9663676416 | bytes 7077888 | tf_op jit(solution)/shard_map/pallas_call | solution.py:240
  68.1 2.8 %shard_map.68 = (f32[4,128]{1,0:T(4,128)}, f32[512,1152]{1,0:T(8,128)}, f32[512,1152]{1,0:T(8,128)}) custom-call(f32[2,512,128]{2,1,0:T(8,128)S(1)} %get-tuple-element.8.loss_acc, f32[2,512,1152]{2,1,0:T(8,128)S(1)} %get-tuple-element.9.grads, bf16[512,1152]{1,0:T(8,128)(2,1)S(1)} %copy-done, bf16[512,1152]{1,0:T(8,128)(2,1)S(1)} %copy-done.1), custom_call_target="tpu_custom_call" | custom-call | flops 9437184 | bytes 4718592 | tf_op jit(solution)/shard_map/pallas_call | solution.py:263
Async XLA Ops:
  1.9 1.3 %copy-start = (bf16[512,1152]{1,0:T(8,128)(2,1)S(1)}, bf16[512,1152]{1,0:T(8,128)(2,1)}, u32[]{:S(2)}) copy-start(bf16[512,1152]{1,0:T(8,128)(2,1)} %image_emb.3) | copy-start | bytes 3538948
  3.2 1.3 %copy-start.1 = (bf16[512,1152]{1,0:T(8,128)(2,1)S(1)}, bf16[512,1152]{1,0:T(8,128)(2,1)}, u32[]{:S(2)}) copy-start(bf16[512,1152]{1,0:T(8,128)(2,1)} %text_emb.3) | copy-start | bytes 3538948
